TPU v7x, 32 devices: a whole 2x2x4 slice. The times are simulated.
32 devices in a mesh: row: 4 (over x, core), col: 8 (over z, y).
Axes of the slice: x: 2, y: 2, z: 4, core: 2. Of those that a mesh axis runs over, the one named last changes fastest.
Arguments:
- a_blocks: float32 [96, 16, 128, 128], P('col', 'row'), may hold values from -0.25 to 0.25
- a_cols: int32 [96, 16], P('col'), may hold values from 0 to 15, as said below
- a_lengths: int32 [96], P('col'), may hold values from 1 to 16, as said below
- b_blocks: float32 [16, 4, 128, 128], P('col', 'row'), may hold values from -6 to 6
- b_cols: int32 [16, 4], P(None, 'row'), may hold values from 0 to 7
- c_cols: int32 [96, 16], P('col', 'row'), may hold values from 0 to 7, as said below
- order: int32 [16], replicated, may hold values from 0 to 15, each once
Outputs:
- c_blocks: float32 [96, 16, 128, 128], P('col', 'row')
Inputs may be any that keep to these rules, and one draw needn't show every extreme that they name: `a_cols`: the 16 entries of one row are distinct. `a_lengths`: the first row has 16 live slots; slots at or after a row's length hold blocks that are not used. `c_cols`: the 4 entries of one row in one row group are distinct. `order`: each number once.
All inputs are finite; a program needn't handle non-finite values.
Results may differ from a plain program's by a relative error of at most 0.0003.
Values sent between devices are 32-bit elements; how exact they have to be, the bound alone decides.
A program may use at most 64 MiB of HBM per device.

v0:
```python
import jax
import jax.numpy as jnp
from jax import lax
from jax.sharding import PartitionSpec as P


def lookup(values_table, indices):
    matched = indices[..., None] == jnp.arange(values_table.shape[0], dtype=jnp.int32)
    return jnp.sum(jnp.where(matched, values_table, 0), axis=-1)


def local(a_blocks, a_cols, a_lengths, b_blocks, b_cols, c_cols, order):
    panels = lax.all_gather(b_blocks, "col", axis=0, tiled=True)[:, 0]
    rows_here, slot_all = a_cols.shape
    pattern_slots = c_cols.shape[1]
    block_size = panels.shape[-1]
    position = lookup(order, a_cols)
    window_col = lookup(b_cols[:, 0], position)
    live_slots = jnp.arange(slot_all, dtype=jnp.int32)[None, :] < a_lengths[:, None]
    weights = ((window_col[:, :, None] == c_cols[:, None, :]) & live_slots[:, :, None]).astype(
        jnp.float32
    )
    zero_sums = jnp.zeros((rows_here, pattern_slots, block_size, block_size), jnp.float32)
    whole_slots = lax.all_gather(a_blocks, "row", axis=1, tiled=True)

    def per_row(row_index, running):
        chosen = jnp.take(panels, position[row_index], axis=0)
        products = jnp.einsum(
            "jab,jbc->jac", whole_slots[row_index], chosen, precision=lax.Precision.HIGHEST
        )
        landed = jnp.einsum(
            "js,jac->sac", weights[row_index], products, precision=lax.Precision.HIGHEST
        )
        return running.at[row_index].add(landed)

    return lax.fori_loop(0, rows_here, per_row, zero_sums)


def solution(mesh):
    return jax.shard_map(
        local,
        mesh=mesh,
        in_specs=(
            P("col", "row", None, None),
            P("col", None),
            P("col"),
            P("col", "row", None, None),
            P(None, "row"),
            P("col", "row"),
            P(),
        ),
        out_specs=P("col", "row", None, None),
        check_vma=False,
    )
```

profile of v0, /device:TPU:1, one launch (start us, length us, event | category | flops | bytes accessed | tf_op | source)
XLA Modules:
  0.0 231.3 jit_solution(10955493273883221862)
XLA Ops:
  9.1 41.7 %all-gather.5.cloned.1.call-done = f32[16,1,128,128]{3,2,1,0:T(8,128)} async-done(((f32[2,1,128,128]{3,2,1,0:T(8,128)}), f32[16,1,128,128]{3,2,1,0:T(8,128)}) %all-gather.5.cloned.1.call-update) | async-done | bytes 1048592 | tf_op jit(solution)/shard_map/all_gather | solution.py:13
  50.8 83.9 %all-gather.3.cloned.1.call-done = f32[12,16,128,128]{3,2,1,0:T(8,128)} async-done(((f32[12,4,128,128]{3,2,1,0:T(8,128)}), f32[12,16,128,128]{3,2,1,0:T(8,128)}) %all-gather.3.cloned.1.call-update) | async-done | bytes 12582928 | tf_op jit(solution)/shard_map/all_gather | solution.py:24
  134.6 2.0 broadcast_in_dim.47.clone
  136.7 87.8 %while.14 = (s32[]{:T(128)}, f32[12,4,128,128]{3,2,1,0:T(8,128)}, f32[12,16,4]{1,2,0:T(4,128)S(1)}, f32[12,16,128,128]{3,2,1,0:T(8,128)}, s32[12,16]{1,0:T(8,128...) while((s32[]{:T(128)}, f32[12,4,128,128]{3,2,1,0:T(8,128)}, ...), condition=%wide.region_4.5_spmd, body=%wide.region_2.4_spmd.sunk | while | flops 415630528 | bytes 7871975 | solution.py:36
  137.4 2.4 %fusion.27 = f32[16,128,128]{2,1,0:T(8,128)S(1)} fusion(f32[16,128,128]{2,1,0:T(8,128)S(1)} %gather_fusion, f32[12,16,128,128]{3,2,1,0:T(8,128)} %get-tuple-element.207, s32[]{:T(128)} %get-tuple-element.195, pred[16]{0:T(512)(128)(4,1)S(1)} %compare_and_fusion.2), kind=kOutput, calls=%fused_computation.4.clone.1 | convolution fusion | flops 402915328 | bytes 3146256 | tf_op jit(solution)/shard_map/while/body/eval_jaxpr/jab,jbc->jac/dot_general | solution.py:28
  140.5 1.0 constant_dynamic-slice_fusion.3
  141.4 1.8 fusion.28
  143.3 0.7 copy_dynamic-update-slice_fusion.2
  144.7 2.4 %fusion.27 = f32[16,128,128]{2,1,0:T(8,128)S(1)} fusion(f32[16,128,128]{2,1,0:T(8,128)S(1)} %gather_fusion, f32[12,16,128,128]{3,2,1,0:T(8,128)} %get-tuple-element.207, s32[]{:T(128)} %get-tuple-element.195, pred[16]{0:T(512)(128)(4,1)S(1)} %compare_and_fusion.2), kind=kOutput, calls=%fused_computation.4.clone.1 | convolution fusion | flops 402915328 | bytes 3146256 | tf_op jit(solution)/shard_map/while/body/eval_jaxpr/jab,jbc->jac/dot_general | solution.py:28
  147.8 1.0 constant_dynamic-slice_fusion.3
  148.8 1.8 fusion.28
  150.6 0.7 copy_dynamic-update-slice_fusion.2
  152.0 2.4 %fusion.27 = f32[16,128,128]{2,1,0:T(8,128)S(1)} fusion(f32[16,128,128]{2,1,0:T(8,128)S(1)} %gather_fusion, f32[12,16,128,128]{3,2,1,0:T(8,128)} %get-tuple-element.207, s32[]{:T(128)} %get-tuple-element.195, pred[16]{0:T(512)(128)(4,1)S(1)} %compare_and_fusion.2), kind=kOutput, calls=%fused_computation.4.clone.1 | convolution fusion | flops 402915328 | bytes 3146256 | tf_op jit(solution)/shard_map/while/body/eval_jaxpr/jab,jbc->jac/dot_general | solution.py:28
  155.1 1.0 constant_dynamic-slice_fusion.3
  156.1 1.8 fusion.28
  157.9 0.7 copy_dynamic-update-slice_fusion.2
  159.3 2.4 %fusion.27 = f32[16,128,128]{2,1,0:T(8,128)S(1)} fusion(f32[16,128,128]{2,1,0:T(8,128)S(1)} %gather_fusion, f32[12,16,128,128]{3,2,1,0:T(8,128)} %get-tuple-element.207, s32[]{:T(128)} %get-tuple-element.195, pred[16]{0:T(512)(128)(4,1)S(1)} %compare_and_fusion.2), kind=kOutput, calls=%fused_computation.4.clone.1 | convolution fusion | flops 402915328 | bytes 3146256 | tf_op jit(solution)/shard_map/while/body/eval_jaxpr/jab,jbc->jac/dot_general | solution.py:28
  162.4 1.0 constant_dynamic-slice_fusion.3
  163.4 1.8 fusion.28
  165.2 0.7 copy_dynamic-update-slice_fusion.2
  166.6 2.4 %fusion.27 = f32[16,128,128]{2,1,0:T(8,128)S(1)} fusion(f32[16,128,128]{2,1,0:T(8,128)S(1)} %gather_fusion, f32[12,16,128,128]{3,2,1,0:T(8,128)} %get-tuple-element.207, s32[]{:T(128)} %get-tuple-element.195, pred[16]{0:T(512)(128)(4,1)S(1)} %compare_and_fusion.2), kind=kOutput, calls=%fused_computation.4.clone.1 | convolution fusion | flops 402915328 | bytes 3146256 | tf_op jit(solution)/shard_map/while/body/eval_jaxpr/jab,jbc->jac/dot_general | solution.py:28
  169.7 1.0 constant_dynamic-slice_fusion.3
  170.7 1.8 fusion.28
  172.5 0.7 copy_dynamic-update-slice_fusion.2
  173.9 2.4 %fusion.27 = f32[16,128,128]{2,1,0:T(8,128)S(1)} fusion(f32[16,128,128]{2,1,0:T(8,128)S(1)} %gather_fusion, f32[12,16,128,128]{3,2,1,0:T(8,128)} %get-tuple-element.207, s32[]{:T(128)} %get-tuple-element.195, pred[16]{0:T(512)(128)(4,1)S(1)} %compare_and_fusion.2), kind=kOutput, calls=%fused_computation.4.clone.1 | convolution fusion | flops 402915328 | bytes 3146256 | tf_op jit(solution)/shard_map/while/body/eval_jaxpr/jab,jbc->jac/dot_general | solution.py:28
  177.0 1.0 constant_dynamic-slice_fusion.3
  178.0 1.8 fusion.28
  179.9 0.7 copy_dynamic-update-slice_fusion.2
  181.2 2.4 %fusion.27 = f32[16,128,128]{2,1,0:T(8,128)S(1)} fusion(f32[16,128,128]{2,1,0:T(8,128)S(1)} %gather_fusion, f32[12,16,128,128]{3,2,1,0:T(8,128)} %get-tuple-element.207, s32[]{:T(128)} %get-tuple-element.195, pred[16]{0:T(512)(128)(4,1)S(1)} %compare_and_fusion.2), kind=kOutput, calls=%fused_computation.4.clone.1 | convolution fusion | flops 402915328 | bytes 3146256 | tf_op jit(solution)/shard_map/while/body/eval_jaxpr/jab,jbc->jac/dot_general | solution.py:28
  184.4 1.0 constant_dynamic-slice_fusion.3
  185.3 1.8 fusion.28
  187.2 0.7 copy_dynamic-update-slice_fusion.2
  188.6 2.4 %fusion.27 = f32[16,128,128]{2,1,0:T(8,128)S(1)} fusion(f32[16,128,128]{2,1,0:T(8,128)S(1)} %gather_fusion, f32[12,16,128,128]{3,2,1,0:T(8,128)} %get-tuple-element.207, s32[]{:T(128)} %get-tuple-element.195, pred[16]{0:T(512)(128)(4,1)S(1)} %compare_and_fusion.2), kind=kOutput, calls=%fused_computation.4.clone.1 | convolution fusion | flops 402915328 | bytes 3146256 | tf_op jit(solution)/shard_map/while/body/eval_jaxpr/jab,jbc->jac/dot_general | solution.py:28
  191.7 1.0 constant_dynamic-slice_fusion.3
  192.6 1.8 fusion.28
  195.9 2.4 %fusion.27 = f32[16,128,128]{2,1,0:T(8,128)S(1)} fusion(f32[16,128,128]{2,1,0:T(8,128)S(1)} %gather_fusion, f32[12,16,128,128]{3,2,1,0:T(8,128)} %get-tuple-element.207, s32[]{:T(128)} %get-tuple-element.195, pred[16]{0:T(512)(128)(4,1)S(1)} %compare_and_fusion.2), kind=kOutput, calls=%fused_computation.4.clone.1 | convolution fusion | flops 402915328 | bytes 3146256 | tf_op jit(solution)/shard_map/while/body/eval_jaxpr/jab,jbc->jac/dot_general | solution.py:28
  199.0 1.0 constant_dynamic-slice_fusion.3
  200.0 1.8 fusion.28
  203.2 2.4 %fusion.27 = f32[16,128,128]{2,1,0:T(8,128)S(1)} fusion(f32[16,128,128]{2,1,0:T(8,128)S(1)} %gather_fusion, f32[12,16,128,128]{3,2,1,0:T(8,128)} %get-tuple-element.207, s32[]{:T(128)} %get-tuple-element.195, pred[16]{0:T(512)(128)(4,1)S(1)} %compare_and_fusion.2), kind=kOutput, calls=%fused_computation.4.clone.1 | convolution fusion | flops 402915328 | bytes 3146256 | tf_op jit(solution)/shard_map/while/body/eval_jaxpr/jab,jbc->jac/dot_general | solution.py:28
  206.3 1.0 constant_dynamic-slice_fusion.3
  207.3 1.8 fusion.28
  210.5 2.4 %fusion.27 = f32[16,128,128]{2,1,0:T(8,128)S(1)} fusion(f32[16,128,128]{2,1,0:T(8,128)S(1)} %gather_fusion, f32[12,16,128,128]{3,2,1,0:T(8,128)} %get-tuple-element.207, s32[]{:T(128)} %get-tuple-element.195, pred[16]{0:T(512)(128)(4,1)S(1)} %compare_and_fusion.2), kind=kOutput, calls=%fused_computation.4.clone.1 | convolution fusion | flops 402915328 | bytes 3146256 | tf_op jit(solution)/shard_map/while/body/eval_jaxpr/jab,jbc->jac/dot_general | solution.py:28
  213.6 1.0 constant_dynamic-slice_fusion.3
  214.6 1.8 fusion.28
  216.4 0.7 copy_dynamic-update-slice_fusion.2
  217.8 2.4 %fusion.27 = f32[16,128,128]{2,1,0:T(8,128)S(1)} fusion(f32[16,128,128]{2,1,0:T(8,128)S(1)} %gather_fusion, f32[12,16,128,128]{3,2,1,0:T(8,128)} %get-tuple-element.207, s32[]{:T(128)} %get-tuple-element.195, pred[16]{0:T(512)(128)(4,1)S(1)} %compare_and_fusion.2), kind=kOutput, calls=%fused_computation.4.clone.1 | convolution fusion | flops 402915328 | bytes 3146256 | tf_op jit(solution)/shard_map/while/body/eval_jaxpr/jab,jbc->jac/dot_general | solution.py:28
  220.9 1.0 constant_dynamic-slice_fusion.3
  221.9 1.8 fusion.28
  (87 shorter events, 21.3 us)
Async XLA Ops:
  6.5 1.5 copy-start.3
  6.5 1.6 copy-start.2
  6.5 1.6 copy-start.4
  6.5 2.0 copy-start.5
  6.5 2.3 %copy-start.6 = (s32[12]{0:T(128)S(1)}, s32[12]{0:T(128)}, u32[]{:S(2)}) copy-start(s32[12]{0:T(128)} %param.13) | copy-start | bytes 148
  6.5 44.2 %all-gather.5.cloned.1.call-start = ((), (), s32[]{:S(2)}) async-start(), calls=%async_computation.1 | async-start | bytes 1179648 | tf_op jit(solution)/shard_map/all_gather | solution.py:13
  7.3 129.4 %copy-start.1 = (s32[4]{0:T(128)S(1)}, s32[4]{0:T(128)}, u32[]{:S(2)}) copy-start(s32[4]{0:T(128)} %constant.90.clone.1) | copy-start | bytes 52
  7.3 127.4 %all-gather.3.cloned.1.call-start = ((), (), s32[]{:S(2)}) async-start(), calls=%async_computation | async-start | bytes 15728640 | tf_op jit(solution)/shard_map/all_gather | solution.py:24
  50.8 85.9 %copy-start = (f32[16,1,128,128]{3,2,1,0:T(8,128)S(1)}, f32[16,1,128,128]{3,2,1,0:T(8,128)}, u32[]{:S(2)}) copy-start(f32[16,1,128,128]{3,2,1,0:T(8,128)} %all-gather.5.cloned.1.call-done) | copy-start | bytes 3145732
Sparse Core Ops, SparseCore 0:
  9.5 41.2 all-gather.4
  52.3 82.2 all-gather.2
where the time goes:
time: 233 us; the launch traced here: 231 us
  waiting for transfers between devices  127 us (55%)
  matrix products  51.1 us (22%)
  local copies, waits for them, and re-layouts  29.9 us (13%)
  between operations  13.5 us (6%)
  other arithmetic  9.43 us (4%)
    all_gather x1, waiting for transfers between devices, local(): whole_slots = lax.all_gather(a_blocks, 'row', axis=1, tiled=True)  83.9 us
    all_gather x1, waiting for transfers between devices, local(): panels = lax.all_gather(b_blocks, 'col', axis=0, tiled=True)[:, 0]  41.7 us
    dot_general x12, matrix products, per_row(): jnp.einsum('jab,jbc->jac', whole_slots[row_index], chosen, precision=lax....  29.1 us
    dot_general x12, matrix products, per_row(): jnp.einsum('js,jac->sac', weights[row_index], products, precision=lax.Pre...  22 us
    another operation x12, local copies, waits for them, and re-layouts  11.6 us
    scatter-add x12, local copies, waits for them, and re-layouts, per_row(): return running.at[row_index].add(landed)  8.72 us
    another operation x12, other arithmetic  8.18 us
    gather x12, local copies, waits for them, and re-layouts, per_row(): chosen = jnp.take(panels, position[row_index], axis=0)  7.37 us
  transfers between devices with their start and end apart: 2, of which 2 were waited for; matrix products, arithmetic and copies ran while one was open for 0% of the time, Pallas kernels for 0%

commit v1 on v0

v1 whole, which is shorter than its diff:
```python
import functools

import jax
import jax.numpy as jnp
from jax import lax
from jax.experimental import pallas as pl
from jax.experimental.pallas import tpu as pltpu
from jax.sharding import PartitionSpec as P

MESH = pl.DeviceIdType.MESH


def kernel(
    n_chip, n_col, chunk, a_cols, a_lengths, b_cols, c_cols, order, a_ref, b_ref, out_ref,
    a_all, b_all, b_split, acc,
    own_sem, out_sem, near_send, near_recv, far_send, far_recv, pass_send, pass_recv, b_send, b_recv,
):
    rows, slots, block = a_ref.shape[0], a_ref.shape[1], a_ref.shape[2]
    pattern = c_cols.shape[1]
    panels_each = b_ref.shape[0]
    panels = b_all.shape[0]
    chunks = rows // chunk
    me, my_col = lax.axis_index("row"), lax.axis_index("col")
    chip, core = me // 2, me % 2
    sibling = chip * 2 + 1 - core
    far = [lax.rem(chip + step, n_chip) * 2 + core for step in range(1, n_chip)]
    far_from = [lax.rem(chip + n_chip - step, n_chip) for step in range(1, n_chip)]
    peers_col = [lax.rem(my_col + step, n_col) for step in range(1, n_col)]
    from_col = [lax.rem(my_col + n_col - step, n_col) for step in range(1, n_col)]

    barrier = pltpu.get_barrier_semaphore()
    for peer in [sibling] + far:
        pl.semaphore_signal(barrier, inc=1, device_id={"row": peer}, device_id_type=MESH)
    for peer in peers_col:
        pl.semaphore_signal(barrier, inc=1, device_id={"col": peer}, device_id_type=MESH)
    pl.semaphore_wait(barrier, n_chip + n_col - 1)

    def part(t):
        return pl.ds(t * chunk, chunk)

    def own_copy():
        return pltpu.make_async_copy(a_ref, a_all.at[me], own_sem.at[0])

    def own_b():
        return pltpu.make_async_copy(b_ref, b_all.at[pl.ds(my_col * panels_each, panels_each)], own_sem.at[1])

    def near_copy(t):
        return pltpu.make_async_remote_copy(
            src_ref=a_ref.at[part(t)], dst_ref=a_all.at[me, part(t)],
            send_sem=near_send.at[t], recv_sem=near_recv.at[t],
            device_id={"row": sibling}, device_id_type=MESH,
        )

    def far_copy(k, t):
        return pltpu.make_async_remote_copy(
            src_ref=a_ref.at[part(t)], dst_ref=a_all.at[me, part(t)],
            send_sem=far_send.at[k, t], recv_sem=far_recv.at[k, t],
            device_id={"row": far[k]}, device_id_type=MESH,
        )

    def pass_copy(k, t):
        source = far_from[k] * 2 + core
        return pltpu.make_async_remote_copy(
            src_ref=a_all.at[source, part(t)], dst_ref=a_all.at[source, part(t)],
            send_sem=pass_send.at[k, t], recv_sem=pass_recv.at[k, t],
            device_id={"row": sibling}, device_id_type=MESH,
        )

    def b_copy(k):
        here = pl.ds(my_col * panels_each, panels_each)
        return pltpu.make_async_remote_copy(
            src_ref=b_ref, dst_ref=b_all.at[here],
            send_sem=b_send.at[k], recv_sem=b_recv.at[k],
            device_id={"col": peers_col[k]}, device_id_type=MESH,
        )

    def out_copy(t):
        return pltpu.make_async_copy(acc.at[part(t)], out_ref.at[part(t)], out_sem.at[t])

    for k in range(n_chip - 1):
        far_copy(k, 0).start()
    for k in range(n_col - 1):
        b_copy(k).start()
    own_b().start()

    @pl.loop(1, chunks)
    def _(t):
        for k in range(n_chip - 1):
            far_copy(k, t).start()

    own_copy().start()

    @pl.loop(0, chunks)
    def _(t):
        near_copy(t).start()

    own_b().wait()
    for k in range(n_col - 1):
        b_copy(k).wait_recv()

    @pl.loop(0, panels)
    def _(p):
        whole = b_all[p]
        high = whole.astype(jnp.bfloat16)
        low = (whole - high.astype(jnp.float32)).astype(jnp.bfloat16)
        both = jnp.concatenate([high, low], axis=1)
        b_split[p, :block, :] = both
        b_split[p, block:, :] = both

    def add_slots(i, source, first):
        products, marks = [], []
        for j in range(slots):
            slot = source * slots + j
            whole = a_all[source, i, j]
            high = whole.astype(jnp.bfloat16)
            low = (whole - high.astype(jnp.float32)).astype(jnp.bfloat16)
            position = order[a_cols[i, slot]]
            window = b_cols[position]
            live = slot < a_lengths[i]
            marks.append([
                jnp.where(jnp.logical_and(live, window == c_cols[i, s]), 1.0, 0.0).astype(jnp.float32)
                for s in range(pattern)
            ])
            wide = jnp.dot(
                jnp.concatenate([high, low], axis=1), b_split[position],
                preferred_element_type=jnp.float32,
            )
            products.append(wide[:, :block] + wide[:, block:])
        for s in range(pattern):
            total = marks[0][s] * products[0]
            for j in range(1, slots):
                total += marks[j][s] * products[j]
            if first:
                acc[i, s] = total
            else:
                acc[i, s] += total

    own_copy().wait()

    @pl.loop(0, chunks)
    def _(t):
        near_copy(t).wait_recv()

        @pl.loop(t * chunk, (t + 1) * chunk)
        def _(i):
            add_slots(i, me, True)
            add_slots(i, sibling, False)

    @pl.loop(0, chunks)
    def _(t):
        for k in range(n_chip - 1):
            far_copy(k, t).wait_recv()
            pass_copy(k, t).start()

        @pl.loop(t * chunk, (t + 1) * chunk)
        def _(i):
            for k in range(n_chip - 1):
                add_slots(i, far_from[k] * 2 + core, False)

        for k in range(n_chip - 1):
            pass_copy(k, t).wait_recv()

        @pl.loop(t * chunk, (t + 1) * chunk)
        def _(i):
            for k in range(n_chip - 1):
                add_slots(i, far_from[k] * 2 + 1 - core, False)

        out_copy(t).start()

    for k in range(n_col - 1):
        b_copy(k).wait_send()

    @pl.loop(0, chunks)
    def _(t):
        near_copy(t).wait_send()
        out_copy(t).wait()
        for k in range(n_chip - 1):
            far_copy(k, t).wait_send()
            pass_copy(k, t).wait_send()


def local(n_chip, n_col, a_blocks, a_cols, a_lengths, b_blocks, b_cols, c_cols, order):
    rows, slots, block = a_blocks.shape[0], a_blocks.shape[1], a_blocks.shape[2]
    pattern = c_cols.shape[1]
    panels_each = b_blocks.shape[0]
    panels = panels_each * n_col
    chunk = max(d for d in range(1, max(1, 4 // slots) + 1) if rows % d == 0)
    chunks = rows // chunk
    smem = pl.BlockSpec(memory_space=pltpu.SMEM)
    hbm = pl.BlockSpec(memory_space=pl.ANY)
    dma = pltpu.SemaphoreType.DMA
    return pl.pallas_call(
        functools.partial(kernel, n_chip, n_col, chunk),
        out_shape=jax.ShapeDtypeStruct((rows, pattern, block, block), jnp.float32),
        in_specs=[smem] * 5 + [hbm] * 2,
        out_specs=hbm,
        scratch_shapes=[
            pltpu.VMEM((n_chip * 2, rows, slots, block, block), jnp.float32),
            pltpu.VMEM((panels, block, block), jnp.float32),
            pltpu.VMEM((panels, 2 * block, 2 * block), jnp.bfloat16),
            pltpu.VMEM((rows, pattern, block, block), jnp.float32),
            dma((2,)),
            dma((chunks,)),
            dma((chunks,)),
            dma((chunks,)),
            dma((n_chip - 1, chunks)),
            dma((n_chip - 1, chunks)),
            dma((n_chip - 1, chunks)),
            dma((n_chip - 1, chunks)),
            dma((n_col - 1,)),
            dma((n_col - 1,)),
        ],
        compiler_params=pltpu.CompilerParams(
            collective_id=0, has_side_effects=True, vmem_limit_bytes=56 * 1024 * 1024
        ),
        cost_estimate=pl.CostEstimate(
            flops=2 * rows * slots * 2 * n_chip * 4 * block**3,
            bytes_accessed=4 * rows * block * block * (slots + pattern),
            transcendentals=0,
        ),
    )(a_cols, a_lengths, b_cols.reshape(-1), c_cols, order, a_blocks, b_blocks.reshape(panels_each, block, block))


def solution(mesh):
    return jax.shard_map(
        functools.partial(local, mesh.shape["row"] // 2, mesh.shape["col"]),
        mesh=mesh,
        in_specs=(
            P("col", "row", None, None),
            P("col", None),
            P("col"),
            P("col", "row", None, None),
            P(None, "row"),
            P("col", "row"),
            P(),
        ),
        out_specs=P("col", "row", None, None),
        check_vma=False,
    )
```

time: 233 us -> 85 us (0.36)
  waiting for transfers between devices: 127 us -> 0 us
  Pallas kernels: 0 us -> 79.5 us
  matrix products: 51.1 us -> 0 us
  local copies, waits for them, and re-layouts: 29.9 us -> 5.27 us
  between operations: 13.5 us -> 0.01 us
  other arithmetic: 9.43 us -> 0 us
    all_gather x2 -> x0, waiting for transfers between devices: 126 us -> none  [the longest x1 83.9 us: local(): whole_slots = lax.all_gather(a_blocks, 'row', axis=1, tiled=True)]
    pallas_call x0 -> x1, Pallas kernels: none -> 79.5 us  [local(): pl.pallas_call(functools.partial(kernel, n_chip, n_col, chunk), out_shape...]
    dot_general x24 -> x0, matrix products: 51.1 us -> none  [the longest x12 29.1 us: per_row(): jnp.einsum('jab,jbc->jac', whole_slots[row_index], chosen, precision=lax....]
    another operation x12 -> x0, local copies, waits for them, and re-layouts: 11.6 us -> none
    scatter-add x12 -> x0, local copies, waits for them, and re-layouts: 8.72 us -> none  [per_row(): return running.at[row_index].add(landed)]
    another operation x12 -> x0, other arithmetic: 8.18 us -> none
    gather x12 -> x0, local copies, waits for them, and re-layouts: 7.37 us -> none  [per_row(): chosen = jnp.take(panels, position[row_index], axis=0)]
    unnamed x15 -> x2, local copies, waits for them, and re-layouts: 0.12 us -> 5.27 us
  transfers between devices with their start and end apart: 2 -> 0, of which waited for: 2 -> 0; matrix products, arithmetic and copies ran while one was open for 0% -> 0% of each run, Pallas kernels for 0% -> 0%
where the time goes in v1:
time: 85 us; the launch traced here: 84.8 us
  Pallas kernels  79.5 us (94%)
  local copies, waits for them, and re-layouts  5.27 us (6%)
    pallas_call x1, Pallas kernels, local(): pl.pallas_call(functools.partial(kernel, n_chip, n_col, chunk), out_shape...  79.5 us
    unnamed x2, local copies, waits for them, and re-layouts  5.27 us

profile of v1, /device:TPU:1, one launch (start us, length us, event | category | flops | bytes accessed | tf_op | source)
XLA Modules:
  0.0 84.8 jit_solution(16685328900527651627)
XLA Ops:
  0.0 1.4 %copy.8.c_cols = s32[12,4]{1,0:T(8,128)} copy(s32[12,4]{0,1:T(4,128)} %param.12) | data formatting | bytes 384 | tf_op args[5]
  1.4 79.5 %shard_map.73 = f32[12,4,128,128]{3,2,1,0:T(8,128)} custom-call(s32[12,16]{1,0:T(8,128)} %a_cols.1, s32[12]{0:T(128)} %a_lengths.1, s32[16]{0:T(128)} %bitcast.3, s32[12,4]{1,0:T(8,128)} %copy.8.c_cols, s32[16]{0:T(128)} %order.1, f32[12,4,128,128]{3,2,1,0:T(8,128)} %a_ref.1, f32[2,128,128]{2,1,0:T(8,128)} %bitcast.2), custom_call_target="tpu_custom_call" | custom-call | flops 3221225472 | bytes 6291456 | tf_op jit(solution)/shard_map/pallas_call | solution.py:192
  80.9 3.9 %copy.10 = f32[12,4,128,128]{3,2,1,0:T(8,128)} copy(f32[12,4,128,128]{3,2,1,0:T(8,128)} %shard_map.73) | data formatting | bytes 6291456

commit v2 on v1

--- a/solution.py
+++ b/solution.py
@@ -11,12 +11,12 @@
 
 
 def kernel(
-    n_chip, n_col, chunk, a_cols, a_lengths, b_cols, c_cols, order, a_ref, b_ref, out_ref,
-    a_all, b_all, b_split, acc,
-    own_sem, out_sem, near_send, near_recv, far_send, far_recv, pass_send, pass_recv, b_send, b_recv,
+    n_chip, n_col, chunk, a_cols, a_lengths, b_cols, c_cols, order, a_ref, b_ref, acc,
+    a_all, b_all, b_split,
+    own_sem, near_send, near_recv, far_send, far_recv, pass_send, pass_recv, b_send, b_recv,
 ):
     rows, slots, block = a_ref.shape[0], a_ref.shape[1], a_ref.shape[2]
-    pattern = c_cols.shape[1]
+    pattern = c_cols.shape[0]
     panels_each = b_ref.shape[0]
     panels = b_all.shape[0]
     chunks = rows // chunk
@@ -74,21 +74,16 @@
             device_id={"col": peers_col[k]}, device_id_type=MESH,
         )
 
-    def out_copy(t):
-        return pltpu.make_async_copy(acc.at[part(t)], out_ref.at[part(t)], out_sem.at[t])
-
-    for k in range(n_chip - 1):
-        far_copy(k, 0).start()
-    for k in range(n_col - 1):
-        b_copy(k).start()
     own_b().start()
-
-    @pl.loop(1, chunks)
-    def _(t):
+    own_copy().start()
+    sent_b = 0
+    for t in range(chunks):
         for k in range(n_chip - 1):
             far_copy(k, t).start()
-
-    own_copy().start()
+        upto = (n_col - 1) * (t + 1) // min(chunks, n_col - 1) if t + 1 < chunks else n_col - 1
+        for k in range(sent_b, min(upto, n_col - 1)):
+            b_copy(k).start()
+        sent_b = min(upto, n_col - 1)
 
     @pl.loop(0, chunks)
     def _(t):
@@ -118,7 +113,7 @@
             window = b_cols[position]
             live = slot < a_lengths[i]
             marks.append([
-                jnp.where(jnp.logical_and(live, window == c_cols[i, s]), 1.0, 0.0).astype(jnp.float32)
+                jnp.where(jnp.logical_and(live, window == c_cols[s, i]), 1.0, 0.0).astype(jnp.float32)
                 for s in range(pattern)
             ])
             wide = jnp.dot(
@@ -165,15 +160,12 @@
             for k in range(n_chip - 1):
                 add_slots(i, far_from[k] * 2 + 1 - core, False)
 
-        out_copy(t).start()
-
     for k in range(n_col - 1):
         b_copy(k).wait_send()
 
     @pl.loop(0, chunks)
     def _(t):
         near_copy(t).wait_send()
-        out_copy(t).wait()
         for k in range(n_chip - 1):
             far_copy(k, t).wait_send()
             pass_copy(k, t).wait_send()
@@ -191,16 +183,14 @@
     dma = pltpu.SemaphoreType.DMA
     return pl.pallas_call(
         functools.partial(kernel, n_chip, n_col, chunk),
-        out_shape=jax.ShapeDtypeStruct((rows, pattern, block, block), jnp.float32),
+        out_shape=pltpu.VMEM((rows, pattern, block, block), jnp.float32),
         in_specs=[smem] * 5 + [hbm] * 2,
-        out_specs=hbm,
+        out_specs=pl.BlockSpec(memory_space=pltpu.VMEM),
         scratch_shapes=[
             pltpu.VMEM((n_chip * 2, rows, slots, block, block), jnp.float32),
             pltpu.VMEM((panels, block, block), jnp.float32),
             pltpu.VMEM((panels, 2 * block, 2 * block), jnp.bfloat16),
-            pltpu.VMEM((rows, pattern, block, block), jnp.float32),
             dma((2,)),
-            dma((chunks,)),
             dma((chunks,)),
             dma((chunks,)),
             dma((n_chip - 1, chunks)),
@@ -211,14 +201,14 @@
             dma((n_col - 1,)),
         ],
         compiler_params=pltpu.CompilerParams(
-            collective_id=0, has_side_effects=True, vmem_limit_bytes=56 * 1024 * 1024
+            collective_id=0, has_side_effects=True, vmem_limit_bytes=60 * 1024 * 1024
         ),
         cost_estimate=pl.CostEstimate(
             flops=2 * rows * slots * 2 * n_chip * 4 * block**3,
             bytes_accessed=4 * rows * block * block * (slots + pattern),
             transcendentals=0,
         ),
-    )(a_cols, a_lengths, b_cols.reshape(-1), c_cols, order, a_blocks, b_blocks.reshape(panels_each, block, block))
+    )(a_cols, a_lengths, b_cols.reshape(-1), c_cols.T, order, a_blocks, b_blocks.reshape(panels_each, block, block))
 
 
 def solution(mesh):

time: 85 us -> 80.5 us (0.947)
  local copies, waits for them, and re-layouts: 5.27 us -> 1.67 us
    unnamed x2 -> x1, local copies, waits for them, and re-layouts: 5.27 us -> 1.67 us
where the time goes in v2:
time: 80.5 us; the launch traced here: 80.4 us
  Pallas kernels  78.7 us (98%)
  local copies, waits for them, and re-layouts  1.67 us (2%)
    pallas_call x1, Pallas kernels, local(): pl.pallas_call(functools.partial(kernel, n_chip, n_col, chunk), out_shape...  78.7 us
    unnamed x1, local copies, waits for them, and re-layouts  1.67 us

profile of v2, /device:TPU:1, one launch (start us, length us, event | category | flops | bytes accessed | tf_op | source)
XLA Modules:
  0.0 80.4 jit_solution(3045562920973729039)
XLA Ops:
  0.0 78.7 %shard_map.73 = f32[12,4,128,128]{3,2,1,0:T(8,128)S(1)} custom-call(s32[12,16]{1,0:T(8,128)} %a_cols.1, s32[12]{0:T(128)} %a_lengths.1, s32[16]{0:T(128)} %bitcast.5, s32[4,12]{1,0:T(4,128)} %bitcast.4, s32[16]{0:T(128)} %order.1, f32[12,4,128,128]{3,2,1,0:T(8,128)} %a_ref.1, f32[2,128,128]{2,1,0:T(8,128)} %bitcast.3), custom_call_target="tpu_custom_call" | custom-call | flops 3221225472 | bytes 6291456 | tf_op jit(solution)/shard_map/pallas_call | solution.py:184
  78.7 1.7 %copy.9 = f32[12,4,128,128]{3,2,1,0:T(8,128)} copy(f32[12,4,128,128]{3,2,1,0:T(8,128)S(1)} %shard_map.73) | data formatting | bytes 6291456

commit v3 on v2

--- a/solution.py
+++ b/solution.py
@@ -8,6 +8,16 @@
 from jax.sharding import PartitionSpec as P
 
 MESH = pl.DeviceIdType.MESH
+
+
+def ring_spot(col, n_col):
+    odd = col % 2
+    return (1 - odd) * (col // 2) + odd * (n_col - 1 - col // 2)
+
+
+def ring_col(spot, n_col):
+    back = spot // (n_col // 2)
+    return (1 - back) * (2 * spot) + back * (2 * (n_col - 1 - spot) + 1)
 
 
 def kernel(
@@ -25,15 +35,16 @@
     sibling = chip * 2 + 1 - core
     far = [lax.rem(chip + step, n_chip) * 2 + core for step in range(1, n_chip)]
     far_from = [lax.rem(chip + n_chip - step, n_chip) for step in range(1, n_chip)]
-    peers_col = [lax.rem(my_col + step, n_col) for step in range(1, n_col)]
-    from_col = [lax.rem(my_col + n_col - step, n_col) for step in range(1, n_col)]
+    spot = ring_spot(my_col, n_col)
+    ring = [ring_col(lax.rem(spot + step, n_col), n_col) for step in (1, n_col - 1)]
+    hops = (n_col // 2, (n_col - 1) // 2)
 
     barrier = pltpu.get_barrier_semaphore()
     for peer in [sibling] + far:
         pl.semaphore_signal(barrier, inc=1, device_id={"row": peer}, device_id_type=MESH)
-    for peer in peers_col:
+    for peer in ring:
         pl.semaphore_signal(barrier, inc=1, device_id={"col": peer}, device_id_type=MESH)
-    pl.semaphore_wait(barrier, n_chip + n_col - 1)
+    pl.semaphore_wait(barrier, n_chip + 2)
 
     def part(t):
         return pl.ds(t * chunk, chunk)
@@ -66,32 +77,40 @@
             device_id={"row": sibling}, device_id_type=MESH,
         )
 
-    def b_copy(k):
-        here = pl.ds(my_col * panels_each, panels_each)
-        return pltpu.make_async_remote_copy(
-            src_ref=b_ref, dst_ref=b_all.at[here],
-            send_sem=b_send.at[k], recv_sem=b_recv.at[k],
-            device_id={"col": peers_col[k]}, device_id_type=MESH,
+    def b_copy(way, hop):
+        back = hop if way == 1 else n_col - hop
+        here = pl.ds(ring_col(lax.rem(spot + back, n_col), n_col) * panels_each, panels_each)
+        return pltpu.make_async_remote_copy(
+            src_ref=b_all.at[here], dst_ref=b_all.at[here],
+            send_sem=b_send.at[way, hop], recv_sem=b_recv.at[way, hop],
+            device_id={"col": ring[way]}, device_id_type=MESH,
         )
 
     own_b().start()
+
+    @pl.loop(0, chunks)
+    def _(t):
+        for k in range(n_chip - 1):
+            far_copy(k, t).start()
+
+    own_b().wait()
+    for way in (0, 1):
+        b_copy(way, 0).start()
     own_copy().start()
-    sent_b = 0
-    for t in range(chunks):
-        for k in range(n_chip - 1):
-            far_copy(k, t).start()
-        upto = (n_col - 1) * (t + 1) // min(chunks, n_col - 1) if t + 1 < chunks else n_col - 1
-        for k in range(sent_b, min(upto, n_col - 1)):
-            b_copy(k).start()
-        sent_b = min(upto, n_col - 1)
 
     @pl.loop(0, chunks)
     def _(t):
         near_copy(t).start()
 
-    own_b().wait()
-    for k in range(n_col - 1):
-        b_copy(k).wait_recv()
+    for way in (0, 1):
+        b_copy(way, 0).wait_recv()
+    for hop in range(1, hops[0]):
+        for way in (0, 1):
+            if hop < hops[way]:
+                b_copy(way, hop).start()
+        for way in (0, 1):
+            if hop < hops[way]:
+                b_copy(way, hop).wait_recv()
 
     @pl.loop(0, panels)
     def _(p):
@@ -160,8 +179,9 @@
             for k in range(n_chip - 1):
                 add_slots(i, far_from[k] * 2 + 1 - core, False)
 
-    for k in range(n_col - 1):
-        b_copy(k).wait_send()
+    for way in (0, 1):
+        for hop in range(hops[way]):
+            b_copy(way, hop).wait_send()
 
     @pl.loop(0, chunks)
     def _(t):
@@ -197,8 +217,8 @@
             dma((n_chip - 1, chunks)),
             dma((n_chip - 1, chunks)),
             dma((n_chip - 1, chunks)),
-            dma((n_col - 1,)),
-            dma((n_col - 1,)),
+            dma((2, n_col // 2)),
+            dma((2, n_col // 2)),
         ],
         compiler_params=pltpu.CompilerParams(
             collective_id=0, has_side_effects=True, vmem_limit_bytes=60 * 1024 * 1024

time: 80.5 us -> 77.6 us (0.964)
  Pallas kernels: 78.7 us -> 75.7 us
    pallas_call x1, Pallas kernels: 78.7 us -> 75.7 us  [local(): pl.pallas_call(functools.partial(kernel, n_chip, n_col, chunk), out_shape...]
where the time goes in v3:
time: 77.6 us; the launch traced here: 77.4 us
  Pallas kernels  75.7 us (98%)
  local copies, waits for them, and re-layouts  1.67 us (2%)
    pallas_call x1, Pallas kernels, local(): pl.pallas_call(functools.partial(kernel, n_chip, n_col, chunk), out_shape...  75.7 us
    unnamed x1, local copies, waits for them, and re-layouts  1.67 us

profile of v3, /device:TPU:1, one launch (start us, length us, event | category | flops | bytes accessed | tf_op | source)
XLA Modules:
  0.0 77.4 jit_solution(11417715120845508326)
XLA Ops:
  0.0 75.7 %shard_map.73 = f32[12,4,128,128]{3,2,1,0:T(8,128)S(1)} custom-call(s32[12,16]{1,0:T(8,128)} %a_cols.1, s32[12]{0:T(128)} %a_lengths.1, s32[16]{0:T(128)} %bitcast.5, s32[4,12]{1,0:T(4,128)} %bitcast.4, s32[16]{0:T(128)} %order.1, f32[12,4,128,128]{3,2,1,0:T(8,128)} %a_ref.1, f32[2,128,128]{2,1,0:T(8,128)} %bitcast.3), custom_call_target="tpu_custom_call" | custom-call | flops 3221225472 | bytes 6291456 | tf_op jit(solution)/shard_map/pallas_call | solution.py:204
  75.7 1.7 %copy.9 = f32[12,4,128,128]{3,2,1,0:T(8,128)} copy(f32[12,4,128,128]{3,2,1,0:T(8,128)S(1)} %shard_map.73) | data formatting | bytes 6291456

commit v4 on v3

--- a/solution.py
+++ b/solution.py
@@ -18,6 +18,20 @@
 def ring_col(spot, n_col):
     back = spot // (n_col // 2)
     return (1 - back) * (2 * spot) + back * (2 * (n_col - 1 - spot) + 1)
+
+
+def cut(rows, slots):
+    pieces, row = [], 0
+    while row < rows - 1:
+        size = (rows - 1 - row + 2) // 3
+        pieces.append((row, size, 0, slots))
+        row += size
+    slot = 0
+    while slot < slots:
+        size = (slots - slot + 1) // 2
+        pieces.append((row, 1, slot, size))
+        slot += size
+    return pieces
 
 
 def kernel(
@@ -62,9 +76,15 @@
             device_id={"row": sibling}, device_id_type=MESH,
         )
 
+    pieces = cut(rows, slots)
+
+    def piece(p):
+        row, row_count, slot, slot_count = pieces[p]
+        return pl.ds(row, row_count), pl.ds(slot, slot_count)
+
     def far_copy(k, t):
         return pltpu.make_async_remote_copy(
-            src_ref=a_ref.at[part(t)], dst_ref=a_all.at[me, part(t)],
+            src_ref=a_ref.at[piece(t)], dst_ref=a_all.at[(me,) + piece(t)],
             send_sem=far_send.at[k, t], recv_sem=far_recv.at[k, t],
             device_id={"row": far[k]}, device_id_type=MESH,
         )
@@ -72,7 +92,7 @@
     def pass_copy(k, t):
         source = far_from[k] * 2 + core
         return pltpu.make_async_remote_copy(
-            src_ref=a_all.at[source, part(t)], dst_ref=a_all.at[source, part(t)],
+            src_ref=a_all.at[(source,) + piece(t)], dst_ref=a_all.at[(source,) + piece(t)],
             send_sem=pass_send.at[k, t], recv_sem=pass_recv.at[k, t],
             device_id={"row": sibling}, device_id_type=MESH,
         )
@@ -88,8 +108,7 @@
 
     own_b().start()
 
-    @pl.loop(0, chunks)
-    def _(t):
+    for t in range(len(pieces)):
         for k in range(n_chip - 1):
             far_copy(k, t).start()
 
@@ -121,9 +140,9 @@
         b_split[p, :block, :] = both
         b_split[p, block:, :] = both
 
-    def add_slots(i, source, first):
+    def add_slots(i, source, first, start=0, count=slots):
         products, marks = [], []
-        for j in range(slots):
+        for j in range(start, start + count):
             slot = source * slots + j
             whole = a_all[source, i, j]
             high = whole.astype(jnp.bfloat16)
@@ -142,7 +161,7 @@
             products.append(wide[:, :block] + wide[:, block:])
         for s in range(pattern):
             total = marks[0][s] * products[0]
-            for j in range(1, slots):
+            for j in range(1, count):
                 total += marks[j][s] * products[j]
             if first:
                 acc[i, s] = total
@@ -160,24 +179,26 @@
             add_slots(i, me, True)
             add_slots(i, sibling, False)
 
-    @pl.loop(0, chunks)
-    def _(t):
+    def add_piece(p, side):
+        row, row_count, slot, slot_count = pieces[p]
+
+        @pl.loop(row, row + row_count)
+        def _(i):
+            for k in range(n_chip - 1):
+                add_slots(i, far_from[k] * 2 + side, False, slot, slot_count)
+
+    for t in range(len(pieces)):
         for k in range(n_chip - 1):
             far_copy(k, t).wait_recv()
             pass_copy(k, t).start()
-
-        @pl.loop(t * chunk, (t + 1) * chunk)
-        def _(i):
+        if t > 0:
             for k in range(n_chip - 1):
-                add_slots(i, far_from[k] * 2 + core, False)
-
-        for k in range(n_chip - 1):
-            pass_copy(k, t).wait_recv()
-
-        @pl.loop(t * chunk, (t + 1) * chunk)
-        def _(i):
-            for k in range(n_chip - 1):
-                add_slots(i, far_from[k] * 2 + 1 - core, False)
+                pass_copy(k, t - 1).wait_recv()
+            add_piece(t - 1, 1 - core)
+        add_piece(t, core)
+    for k in range(n_chip - 1):
+        pass_copy(k, len(pieces) - 1).wait_recv()
+    add_piece(len(pieces) - 1, 1 - core)
 
     for way in (0, 1):
         for hop in range(hops[way]):
@@ -186,6 +207,8 @@
     @pl.loop(0, chunks)
     def _(t):
         near_copy(t).wait_send()
+
+    for t in range(len(pieces)):
         for k in range(n_chip - 1):
             far_copy(k, t).wait_send()
             pass_copy(k, t).wait_send()
@@ -213,10 +236,10 @@
             dma((2,)),
             dma((chunks,)),
             dma((chunks,)),
-            dma((n_chip - 1, chunks)),
-            dma((n_chip - 1, chunks)),
-            dma((n_chip - 1, chunks)),
-            dma((n_chip - 1, chunks)),
+            dma((n_chip - 1, len(cut(rows, slots)))),
+            dma((n_chip - 1, len(cut(rows, slots)))),
+            dma((n_chip - 1, len(cut(rows, slots)))),
+            dma((n_chip - 1, len(cut(rows, slots)))),
             dma((2, n_col // 2)),
             dma((2, n_col // 2)),
         ],

time: 77.6 us -> 77.1 us (level)
  no operation moved by 1% of the time
where the time goes in v4:
time: 77.1 us; the launch traced here: 76.9 us
  Pallas kernels  75.2 us (98%)
  local copies, waits for them, and re-layouts  1.67 us (2%)
    pallas_call x1, Pallas kernels, local(): pl.pallas_call(functools.partial(kernel, n_chip, n_col, chunk), out_shape...  75.2 us
    unnamed x1, local copies, waits for them, and re-layouts  1.67 us

profile of v4, /device:TPU:1, one launch (start us, length us, event | category | flops | bytes accessed | tf_op | source)
XLA Modules:
  0.0 76.9 jit_solution(12559755798813247996)
XLA Ops:
  0.0 75.2 %shard_map.73 = f32[12,4,128,128]{3,2,1,0:T(8,128)S(1)} custom-call(s32[12,16]{1,0:T(8,128)} %a_cols.1, s32[12]{0:T(128)} %a_lengths.1, s32[16]{0:T(128)} %bitcast.5, s32[4,12]{1,0:T(4,128)} %bitcast.4, s32[16]{0:T(128)} %order.1, f32[12,4,128,128]{3,2,1,0:T(8,128)} %a_ref.1, f32[2,128,128]{2,1,0:T(8,128)} %bitcast.3), custom_call_target="tpu_custom_call" | custom-call | flops 3221225472 | bytes 6291456 | tf_op jit(solution)/shard_map/pallas_call | solution.py:227
  75.2 1.7 %copy.9 = f32[12,4,128,128]{3,2,1,0:T(8,128)} copy(f32[12,4,128,128]{3,2,1,0:T(8,128)S(1)} %shard_map.73) | data formatting | bytes 6291456

commit v5 on v4

--- a/solution.py
+++ b/solution.py
@@ -71,7 +71,7 @@
 
     def near_copy(t):
         return pltpu.make_async_remote_copy(
-            src_ref=a_ref.at[part(t)], dst_ref=a_all.at[me, part(t)],
+            src_ref=a_all.at[me, part(t)], dst_ref=a_all.at[me, part(t)],
             send_sem=near_send.at[t], recv_sem=near_recv.at[t],
             device_id={"row": sibling}, device_id_type=MESH,
         )
@@ -84,7 +84,7 @@
 
     def far_copy(k, t):
         return pltpu.make_async_remote_copy(
-            src_ref=a_ref.at[piece(t)], dst_ref=a_all.at[(me,) + piece(t)],
+            src_ref=a_ref.at[piece(t)] if t == 0 else a_all.at[(me,) + piece(t)], dst_ref=a_all.at[(me,) + piece(t)],
             send_sem=far_send.at[k, t], recv_sem=far_recv.at[k, t],
             device_id={"row": far[k]}, device_id_type=MESH,
         )
@@ -108,14 +108,16 @@
 
     own_b().start()
 
-    for t in range(len(pieces)):
-        for k in range(n_chip - 1):
-            far_copy(k, t).start()
-
+    own_copy().start()
+    for k in range(n_chip - 1):
+        far_copy(k, 0).start()
     own_b().wait()
     for way in (0, 1):
         b_copy(way, 0).start()
-    own_copy().start()
+    own_copy().wait()
+    for t in range(1, len(pieces)):
+        for k in range(n_chip - 1):
+            far_copy(k, t).start()
 
     @pl.loop(0, chunks)
     def _(t):
@@ -168,8 +170,6 @@
             else:
                 acc[i, s] += total
 
-    own_copy().wait()
-
     @pl.loop(0, chunks)
     def _(t):
         near_copy(t).wait_recv()

time: 77.1 us -> 77.1 us (level)
  no operation moved by 1% of the time
where the time goes in v5:
time: 77.1 us; the launch traced here: 76.9 us
  Pallas kernels  75.2 us (98%)
  local copies, waits for them, and re-layouts  1.67 us (2%)
    pallas_call x1, Pallas kernels, local(): pl.pallas_call(functools.partial(kernel, n_chip, n_col, chunk), out_shape...  75.2 us
    unnamed x1, local copies, waits for them, and re-layouts  1.67 us

profile of v5, /device:TPU:1, one launch (start us, length us, event | category | flops | bytes accessed | tf_op | source)
XLA Modules:
  0.0 76.9 jit_solution(7774839930197398330)
XLA Ops:
  0.0 75.2 %shard_map.73 = f32[12,4,128,128]{3,2,1,0:T(8,128)S(1)} custom-call(s32[12,16]{1,0:T(8,128)} %a_cols.1, s32[12]{0:T(128)} %a_lengths.1, s32[16]{0:T(128)} %bitcast.5, s32[4,12]{1,0:T(4,128)} %bitcast.4, s32[16]{0:T(128)} %order.1, f32[12,4,128,128]{3,2,1,0:T(8,128)} %a_ref.1, f32[2,128,128]{2,1,0:T(8,128)} %bitcast.3), custom_call_target="tpu_custom_call" | custom-call | flops 3221225472 | bytes 6291456 | tf_op jit(solution)/shard_map/pallas_call | solution.py:227
  75.3 1.7 %copy.9 = f32[12,4,128,128]{3,2,1,0:T(8,128)} copy(f32[12,4,128,128]{3,2,1,0:T(8,128)S(1)} %shard_map.73) | data formatting | bytes 6291456

commit v6 on v5

--- a/solution.py
+++ b/solution.py
@@ -214,6 +214,15 @@
             pass_copy(k, t).wait_send()
 
 
+def write_kernel(sums, out_ref, sem):
+    rows = sums.shape[0]
+    copies = [pltpu.make_async_copy(sums.at[i], out_ref.at[i], sem.at[i]) for i in range(rows)]
+    for copy in copies:
+        copy.start()
+    for copy in copies:
+        copy.wait()
+
+
 def local(n_chip, n_col, a_blocks, a_cols, a_lengths, b_blocks, b_cols, c_cols, order):
     rows, slots, block = a_blocks.shape[0], a_blocks.shape[1], a_blocks.shape[2]
     pattern = c_cols.shape[1]
@@ -224,7 +233,7 @@
     smem = pl.BlockSpec(memory_space=pltpu.SMEM)
     hbm = pl.BlockSpec(memory_space=pl.ANY)
     dma = pltpu.SemaphoreType.DMA
-    return pl.pallas_call(
+    sums = pl.pallas_call(
         functools.partial(kernel, n_chip, n_col, chunk),
         out_shape=pltpu.VMEM((rows, pattern, block, block), jnp.float32),
         in_specs=[smem] * 5 + [hbm] * 2,
@@ -252,6 +261,14 @@
             transcendentals=0,
         ),
     )(a_cols, a_lengths, b_cols.reshape(-1), c_cols.T, order, a_blocks, b_blocks.reshape(panels_each, block, block))
+    return pl.pallas_call(
+        write_kernel,
+        out_shape=jax.ShapeDtypeStruct(sums.shape, sums.dtype),
+        in_specs=[pl.BlockSpec(memory_space=pltpu.VMEM)],
+        out_specs=hbm,
+        scratch_shapes=[dma((rows,))],
+        compiler_params=pltpu.CompilerParams(vmem_limit_bytes=60 * 1024 * 1024),
+    )(pltpu.with_memory_space_constraint(sums, pltpu.VMEM))
 
 
 def solution(mesh):

time: 77.1 us -> 77.2 us (level)
  Pallas kernels: 75.2 us -> 77 us
  local copies, waits for them, and re-layouts: 1.67 us -> 0 us
    pallas_call x0 -> x1, Pallas kernels: none -> 1.76 us  [local(): pl.pallas_call(write_kernel, out_shape=jax.ShapeDtypeStruct(sums.shape, s...]
    unnamed x1 -> x0, local copies, waits for them, and re-layouts: 1.67 us -> none
where the time goes in v6:
time: 77.2 us; the launch traced here: 77 us
  Pallas kernels  77 us (100%)
    pallas_call x1, Pallas kernels, local(): pl.pallas_call(functools.partial(kernel, n_chip, n_col, chunk), out_shape...  75.2 us
    pallas_call x1, Pallas kernels, local(): pl.pallas_call(write_kernel, out_shape=jax.ShapeDtypeStruct(sums.shape, s...  1.76 us

profile of v6, /device:TPU:1, one launch (start us, length us, event | category | flops | bytes accessed | tf_op | source)
XLA Modules:
  0.0 77.0 jit_solution(4816595238198023535)
XLA Ops:
  0.0 75.2 %shard_map.73.sums = f32[12,4,128,128]{3,2,1,0:T(8,128)S(1)} custom-call(s32[12,16]{1,0:T(8,128)} %a_cols.1, s32[12]{0:T(128)} %a_lengths.1, s32[16]{0:T(128)} %bitcast.5, s32[4,12]{1,0:T(4,128)} %bitcast.4, s32[16]{0:T(128)} %order.1, f32[12,4,128,128]{3,2,1,0:T(8,128)} %a_ref.1, f32[2,128,128]{2,1,0:T(8,128)} %bitcast.3), custom_call_target="tpu_custom_call" | custom-call | flops 3221225472 | bytes 6291456 | tf_op jit(solution)/shard_map/pallas_call | solution.py:236
  75.3 1.8 %shard_map.74 = f32[12,4,128,128]{3,2,1,0:T(8,128)} custom-call(f32[12,4,128,128]{3,2,1,0:T(8,128)S(1)} %shard_map.73.sums), custom_call_target="tpu_custom_call" | custom-call | tf_op jit(solution)/shard_map/pallas_call | solution.py:264
